TPU v7x, 32 devices: a whole 2x2x4 slice. The times are simulated.
32 devices in a mesh: section: 4 (over x, core), seq: 2 (over y), dp: 4 (over z).
Axes of the slice: x: 2, y: 2, z: 4, core: 2. Of those that a mesh axis runs over, the one named last changes fastest.
Arguments:
- act_rows: bfloat16 [4, 4, 128, 4096], P('section', 'dp', 'seq'), may hold values from -30 to 30
- mem_rows: bfloat16 [4, 4, 128, 4096], P('section', 'dp', 'seq'), may hold values from -30 to 30
- w_query: bfloat16 [4, 4096, 4096], P('section', 'dp', 'seq'), may hold values from -8 to 8
- w_key: bfloat16 [4, 4096, 4096], P('section', 'dp', 'seq'), may hold values from -8 to 8
- w_value: bfloat16 [4, 4096, 4096], P('section', 'dp', 'seq'), may hold values from -0.09375 to 0.09375
- w_out: bfloat16 [4, 4096, 4096], P('section', ('seq', 'dp')), may hold values from -0.09375 to 0.09375
- ln_gain: float32 [4, 4096], P('section'), may hold values from 0.5 to 1.5
- final_gain: float32 [4096], replicated, may hold values from 0.5 to 1.5
- src_len: int32 [4, 4], P('section', 'dp'), may hold values from 32 to 128
- tgt_len: int32 [4, 4], P('section', 'dp'), may hold values from 32 to 128
Outputs:
- act_next: bfloat16 [4, 4, 128, 4096], P('section', 'dp', 'seq')
- mem_next: bfloat16 [4, 4, 128, 4096], P('section', 'dp', 'seq')
All inputs are finite; a program needn't handle non-finite values.
Results may differ from a plain program's by a relative error of at most 0.013.
The roundings to bfloat16 on the way count: a program that leaves them out, or rounds other values in their place, can miss the bound.
Values may be sent and summed in bfloat16 or wider, within the bound.
A program may use at most 128 MiB of HBM per device.

v0:
```python
import functools

import jax
import jax.numpy as jnp
from jax import lax
from jax.experimental import pallas as pl
from jax.experimental.pallas import tpu as pltpu
from jax.sharding import PartitionSpec as P

HEAD_DIM = 64


EPS = 1e-06


def passed_along(x, axis, by):
    count = lax.axis_size(axis)
    return lax.ppermute(x, axis, [(i, (i + by) % count) for i in range(count)])


def normed(rows, gain):
    values = rows.astype(jnp.float32)
    scaled = values * lax.rsqrt(jnp.mean(values * values, axis=-1, keepdims=True) + EPS)
    return (scaled * gain).astype(jnp.bfloat16)


def attend(queries, keys, values, src_len):
    seqs, total_rows, width = queries.shape
    head_count = width // HEAD_DIM
    shape = (seqs, total_rows, head_count, HEAD_DIM)
    queries, keys, values = (a.reshape(shape) for a in (queries, keys, values))
    visible = jnp.arange(total_rows, dtype=jnp.int32)[None, :] < src_len[:, None]
    scores = jnp.einsum(
        "bqhd,bkhd->bhqk", queries, keys, preferred_element_type=jnp.float32
    ) * HEAD_DIM ** (-0.5)
    scores = jnp.where(visible[:, None, None, :], scores, -1e30)
    top_score = jnp.max(scores, axis=-1, keepdims=True)
    raw_weights = jnp.exp(scores - top_score)
    weights = (raw_weights / jnp.sum(raw_weights, axis=-1, keepdims=True)).astype(jnp.bfloat16)
    heads = jnp.einsum("bhqk,bkhd->bqhd", weights, values, preferred_element_type=jnp.float32)
    return heads.astype(jnp.bfloat16).reshape(seqs, total_rows, width)


def per_device(
    act_rows, mem_rows, w_query, w_key, w_value, w_out, ln_gain, final_gain, src_len, tgt_len
):
    is_first = lax.axis_index("section") == 0
    seqs = lax.axis_size("dp")
    halves = lax.axis_size("seq")
    act_here = act_rows[0, 0]
    mem_here = mem_rows[0, 0]
    rows_here, width = act_here.shape
    gain = ln_gain[0]
    depth, cols = w_query.shape[1:]
    own = cols // seqs
    rows_in = jnp.where(is_first, mem_here, act_here)
    query_in = normed(rows_in, gain)
    source_in = jnp.where(is_first, query_in, mem_here)
    both = jnp.stack([query_in, source_in]).reshape(2, rows_here, seqs, depth)
    both = lax.all_to_all(both.transpose(2, 0, 1, 3), "dp", 0, 0, tiled=True)
    both = lax.all_gather(both, "seq", axis=0, tiled=False)
    both = both.transpose(2, 1, 0, 3, 4).reshape(2, seqs * halves * rows_here, depth)
    total = seqs * halves * rows_here

    def project(rows, weight):
        part = jnp.dot(rows, weight[0], preferred_element_type=jnp.float32).astype(jnp.bfloat16)
        part = part.reshape(total, seqs, own).transpose(1, 0, 2)
        part = lax.psum_scatter(part, "dp", scatter_dimension=0, tiled=False)
        return part.reshape(seqs, halves * rows_here, own)

    queries = project(both[0], w_query)
    keys = project(both[1], w_key)
    values = project(both[1], w_value)
    lengths = lax.all_gather(src_len[0], "dp", axis=0, tiled=True)
    heads_out = attend(queries, keys, values, lengths)
    update = jnp.dot(
        heads_out.reshape(total, own), w_out[0], preferred_element_type=jnp.float32
    ).astype(jnp.bfloat16).reshape(seqs, halves, rows_here, width)
    update = lax.psum_scatter(update, "seq", scatter_dimension=1, tiled=False)
    update = lax.psum_scatter(update, "dp", scatter_dimension=0, tiled=False).astype(jnp.float32)
    residual = rows_in.astype(jnp.float32)
    positions = lax.axis_index("seq") * rows_here + jnp.arange(rows_here, dtype=jnp.int32)
    keep_rows = (positions < tgt_len[0, 0])[:, None]
    decoded = (residual + jnp.where(keep_rows, update, jnp.float32(0.0))).astype(jnp.bfloat16)
    encoded = normed(residual + update, final_gain)
    emit_act = jnp.where(is_first, act_here, decoded)
    emit_mem = jnp.where(is_first, encoded, mem_here)
    next_act, next_mem = passed_along((emit_act, emit_mem), "section", 1)
    return (next_act[None, None], next_mem[None, None])


ROW_BLOCK = 16
LANES = 128
AHEAD = 2
OUT_CHUNK = 1024
VMEM_BYTES = 60 * 1024 * 1024
BF16 = jnp.bfloat16
F32 = jnp.float32


def scratch_of(seqs, rows, width, depth, cols):
    own, tokens = cols // seqs, 2 * rows
    vmem = {
        "weights": ((3, depth, cols), BF16),
        "w_out": ((own, width), BF16),
        "cut": ((2, seqs, rows, depth), BF16),
        "x": ((2, seqs, 2, rows, depth), BF16),
        "bias": ((seqs, 8, tokens), F32),
        "other": ((rows, width), BF16),
        "part": ((seqs, seqs, 3, tokens, own), BF16),
        "mine": ((seqs, 3, tokens, own), F32),
        "got": ((seqs, seqs - 1, 3, tokens, own), BF16),
        "qkv": ((3, tokens, own), BF16),
        "heads": ((tokens, own), BF16),
        "half": ((seqs, rows, width), F32),
        "y_out": ((seqs, rows, width), BF16),
        "y_in": ((seqs, rows, width), BF16),
        "z_out": ((seqs, rows, width), BF16),
        "z_in": ((seqs, rows, width), BF16),
        "late": ((rows, width), BF16),
    }
    sems = {
        "load": (4,),
        "cut_s": (2, seqs), "cut_r": (2, seqs),
        "fwd_s": (2, seqs), "fwd_r": (2, seqs),
        "bias_s": (seqs,), "bias_r": (seqs,),
        "part_s": (seqs, seqs - 1), "part_r": (seqs, seqs - 1),
        "y_s": (seqs,), "y_r": (seqs,),
        "z_s": (seqs,), "z_r": (seqs,),
        "hand_s": (2,), "hand_r": (2,),
    }
    return vmem, sems


def fits(seqs, halves, rows, width, depth, cols):
    own = cols // seqs
    if halves != 2 or rows % ROW_BLOCK or own % LANES or depth % LANES or width % OUT_CHUNK:
        return False
    vmem, _ = scratch_of(seqs, rows, width, depth, cols)
    total = 8 * rows * width * 2
    for shape, dtype in vmem.values():
        count = jnp.dtype(dtype).itemsize
        for extent in shape:
            count *= extent
        total += count
    return total <= VMEM_BYTES - 2 * 1024 * 1024


def tick_kernel(
    names, act, mem, w_q, w_k, w_v, w_o, gain, last_gain, src_len, tgt_len, early_out, late_out, *scratch
):
    refs = dict(zip(names, scratch))
    weights, w_out, cut, x, bias = (refs[n] for n in ("weights", "w_out", "cut", "x", "bias"))
    seqs, rows, depth = cut.shape[1:]
    width = act.shape[1]
    tokens = 2 * rows
    own = w_out.shape[0]
    sections = lax.axis_size("section")
    section = lax.axis_index("section")
    side = lax.axis_index("seq")
    me = lax.axis_index("dp")
    is_first = section == 0
    ahead = lax.rem(section + 1, sections)
    behind = lax.rem(section + sections - 1, sections)

    def remote(source, target, send, recv, device):
        return pltpu.make_async_remote_copy(
            src_ref=source, dst_ref=target, send_sem=send, recv_sem=recv,
            device_id=device, device_id_type=pl.DeviceIdType.MESH,
        )

    barrier = pltpu.get_barrier_semaphore()
    for step in range(1, seqs):
        pl.semaphore_signal(
            barrier, inc=1, device_id={"dp": lax.rem(me + step, seqs)},
            device_id_type=pl.DeviceIdType.MESH,
        )
    for device in ({"seq": 1 - side}, {"section": ahead}, {"section": behind}):
        pl.semaphore_signal(barrier, inc=1, device_id=device, device_id_type=pl.DeviceIdType.MESH)

    loads = [
        pltpu.make_async_copy(w_q, weights.at[0], refs["load"].at[0]),
        pltpu.make_async_copy(w_k, weights.at[1], refs["load"].at[1]),
        pltpu.make_async_copy(w_v, weights.at[2], refs["load"].at[2]),
        pltpu.make_async_copy(w_o, w_out, refs["load"].at[3]),
    ]
    for load in loads:
        load.start()

    def residual_rows(at):
        return jnp.where(is_first, mem[at, :], act[at, :]).astype(F32)

    def norm_block(r, carry):
        at = pl.ds(pl.multiple_of(r * ROW_BLOCK, ROW_BLOCK), ROW_BLOCK)
        query_in = normed(residual_rows(at), gain[...])
        source_in = jnp.where(is_first, query_in, mem[at, :])
        refs["other"][at, :] = jnp.where(is_first, act[at, :], mem[at, :])
        for j in range(seqs):
            cut[0, j, at, :] = query_in[:, j * depth:(j + 1) * depth]
            cut[1, j, at, :] = source_in[:, j * depth:(j + 1) * depth]
        return carry

    lax.fori_loop(0, rows // ROW_BLOCK, norm_block, 0)
    place = lax.broadcasted_iota(jnp.int32, (8, tokens), 1)
    bias[me] = jnp.where(place < src_len[0, 0], jnp.float32(0.0), jnp.float32(-1e30))
    pl.semaphore_wait(barrier, seqs + 2)

    def cut_copy(kind, to):
        return remote(
            cut.at[kind, to], x.at[kind, me, side], refs["cut_s"].at[kind, to],
            refs["cut_r"].at[kind, me], {"dp": to},
        )

    def bias_copy(to):
        return remote(
            bias.at[me], bias.at[me], refs["bias_s"].at[to], refs["bias_r"].at[me], {"dp": to}
        )

    for kind in (1, 0):
        for step in range(1, seqs):
            cut_copy(kind, lax.rem(me + step, seqs)).start()
    for step in range(1, seqs):
        bias_copy(lax.rem(me + step, seqs)).start()
    early = remote(
        refs["other"], early_out, refs["hand_s"].at[0], refs["hand_r"].at[0], {"section": ahead}
    )
    early.start()
    x[0, me, side] = cut[0, me]
    x[1, me, side] = cut[1, me]

    def fwd_copy(kind, b, half):
        return remote(
            x.at[kind, b, half], x.at[kind, b, half], refs["fwd_s"].at[kind, b],
            refs["fwd_r"].at[kind, b], {"seq": 1 - side},
        )

    def forward(b):
        @pl.when(b != me)
        def _():
            for kind in (1, 0):
                remote(
                    cut.at[kind, b], x.at[kind, b, side], refs["cut_s"].at[kind, b],
                    refs["cut_r"].at[kind, b], {"dp": b},
                ).wait_recv()
                fwd_copy(kind, b, side).start()

        @pl.when(b == me)
        def _():
            for kind in (1, 0):
                fwd_copy(kind, b, side).start()

    def part_copy(b, step):
        to = lax.rem(me + step, seqs)
        return remote(
            refs["part"].at[b, to], refs["got"].at[b, step - 1], refs["part_s"].at[b, step - 1],
            refs["part_r"].at[b, step - 1], {"dp": to},
        )

    def project(b):
        for kind in (1, 0):
            fwd_copy(kind, b, 1 - side).wait_recv()
        for step in list(range(1, seqs)) + [0]:
            to = lax.rem(me + step, seqs)
            at = pl.ds(pl.multiple_of(to * own, own), own)
            for which in range(3):
                product = jnp.dot(
                    x[min(which, 1), b].reshape(tokens, depth), weights[which, :, at],
                    preferred_element_type=F32,
                )
                if step:
                    refs["part"][b, to, which] = product.astype(BF16)
                else:
                    refs["mine"][b, which] = product
            if step:
                part_copy(b, step).start()

    def y_copy(b):
        return remote(
            refs["y_out"].at[b], refs["y_in"].at[b], refs["y_s"].at[b], refs["y_r"].at[b],
            {"seq": 1 - side},
        )

    def attend_one(b):
        for step in range(1, seqs):
            part_copy(b, step).wait_recv()

        @pl.when(b != me)
        def _():
            remote(
                bias.at[b], bias.at[b], refs["bias_s"].at[b], refs["bias_r"].at[b], {"dp": b}
            ).wait_recv()

        for which in range(3):
            total = refs["mine"][b, which]
            for step in range(seqs - 1):
                total += refs["got"][b, step, which].astype(F32)
            refs["qkv"][which] = total.astype(BF16)
        hide = bias[b][0:1, :]
        lane = lax.broadcasted_iota(jnp.int32, (1, LANES), 1)
        group = LANES // HEAD_DIM
        for pair in range(own // LANES):
            at = pl.ds(pair * LANES, LANES)
            query, key, value = (refs["qkv"][which, :, at] for which in range(3))
            result = None
            for h in range(group):
                inside = (lane >= h * HEAD_DIM) & (lane < (h + 1) * HEAD_DIM)
                scores = lax.dot_general(
                    jnp.where(inside, query, jnp.bfloat16(0.0)), key, (((1,), (1,)), ((), ())),
                    preferred_element_type=F32,
                ) * HEAD_DIM ** (-0.5) + hide
                raw = jnp.exp(scores - jnp.max(scores, axis=-1, keepdims=True))
                soft = (raw / jnp.sum(raw, axis=-1, keepdims=True)).astype(BF16)
                out = jnp.dot(soft, value, preferred_element_type=F32)
                result = out if result is None else jnp.where(inside, out, result)
            refs["heads"][:, at] = result.astype(BF16)
        heads = refs["heads"][...]
        for start in range(0, width, OUT_CHUNK):
            at = pl.ds(start, OUT_CHUNK)
            product = jnp.dot(heads, w_out[:, at], preferred_element_type=F32)
            low, high = product[:rows], product[rows:]
            refs["half"][b, :, at] = jnp.where(side == 0, low, high)
            refs["y_out"][b, :, at] = jnp.where(side == 0, high, low).astype(BF16)
        y_copy(b).start()

    def z_copy(b):
        return remote(
            refs["z_out"].at[b], refs["z_in"].at[me], refs["z_s"].at[b], refs["z_r"].at[me],
            {"dp": b},
        )

    def hand_over(b):
        y_copy(b).wait_recv()

        @pl.when(b != me)
        def _():
            refs["z_out"][b] = (refs["half"][b] + refs["y_in"][b].astype(F32)).astype(BF16)
            z_copy(b).start()

    forward(0)

    def turn(t, carry):
        @pl.when(t < seqs - 1)
        def _():
            forward(t + 1)

        @pl.when(t == 0)
        def _():
            for load in loads:
                load.wait()

        @pl.when(t < seqs)
        def _():
            project(t)

        @pl.when((t >= AHEAD) & (t < seqs + AHEAD))
        def _():
            attend_one(t - AHEAD)

        @pl.when(t >= AHEAD + 1)
        def _():
            hand_over(t - AHEAD - 1)

        return carry

    lax.fori_loop(0, seqs + AHEAD + 1, turn, 0)

    for step in range(1, seqs):
        b = lax.rem(me + step, seqs)
        remote(
            refs["z_out"].at[b], refs["z_in"].at[b], refs["z_s"].at[b], refs["z_r"].at[b],
            {"dp": b},
        ).wait_recv()

    def final_block(r, carry):
        at = pl.ds(pl.multiple_of(r * ROW_BLOCK, ROW_BLOCK), ROW_BLOCK)
        update = refs["half"][me, at, :] + refs["y_in"][me, at, :].astype(F32)
        for step in range(1, seqs):
            update += refs["z_in"][lax.rem(me + step, seqs), at, :].astype(F32)
        residual = residual_rows(at)
        place = side * rows + r * ROW_BLOCK + lax.broadcasted_iota(jnp.int32, (ROW_BLOCK, 1), 0)
        kept = jnp.where(place < tgt_len[0, 0], update, jnp.float32(0.0))
        decoded = (residual + kept).astype(BF16)
        encoded = normed(residual + update, last_gain[...])
        refs["late"][at, :] = jnp.where(is_first, encoded, decoded)
        return carry

    lax.fori_loop(0, rows // ROW_BLOCK, final_block, 0)
    late = remote(
        refs["late"], late_out, refs["hand_s"].at[1], refs["hand_r"].at[1], {"section": ahead}
    )
    late.start()

    for step in range(1, seqs):
        b = lax.rem(me + step, seqs)
        for kind in range(2):
            cut_copy(kind, b).wait_send()
        bias_copy(b).wait_send()
        z_copy(b).wait_send()

    def drain(b, carry):
        for kind in range(2):
            fwd_copy(kind, b, side).wait_send()
        for step in range(1, seqs):
            part_copy(b, step).wait_send()
        y_copy(b).wait_send()
        return carry

    lax.fori_loop(0, seqs, drain, 0)
    early.wait()
    late.wait()


def one_kernel(
    act_rows, mem_rows, w_query, w_key, w_value, w_out, ln_gain, final_gain, src_len, tgt_len
):
    rows, width = act_rows.shape[2:]
    depth, cols = w_query.shape[1:]
    seqs = lax.axis_size("dp")
    vmem, sems = scratch_of(seqs, rows, width, depth, cols)
    in_vmem = pl.BlockSpec(memory_space=pltpu.VMEM)
    in_hbm = pl.BlockSpec(memory_space=pl.ANY)
    in_smem = pl.BlockSpec(memory_space=pltpu.SMEM)
    out = jax.ShapeDtypeStruct((rows, width), BF16)
    total = 2 * rows * seqs
    early, late = pl.pallas_call(
        functools.partial(tick_kernel, tuple(vmem) + tuple(sems)),
        out_shape=(out, out),
        in_specs=[in_vmem] * 2 + [in_hbm] * 4 + [in_vmem] * 2 + [in_smem] * 2,
        out_specs=(in_vmem, in_vmem),
        scratch_shapes=[pltpu.VMEM(*spec) for spec in vmem.values()]
        + [pltpu.SemaphoreType.DMA(shape) for shape in sems.values()],
        compiler_params=pltpu.CompilerParams(
            collective_id=0, has_side_effects=True, vmem_limit_bytes=VMEM_BYTES
        ),
        cost_estimate=pl.CostEstimate(
            flops=8 * total * depth * cols, bytes_accessed=8 * depth * cols, transcendentals=0
        ),
    )(
        act_rows[0, 0], mem_rows[0, 0], w_query[0], w_key[0], w_value[0], w_out[0],
        ln_gain, final_gain[None], src_len, tgt_len,
    )
    from_first = lax.axis_index("section") == 1
    next_act = jnp.where(from_first, early, late)
    next_mem = jnp.where(from_first, late, early)
    return (next_act[None, None], next_mem[None, None])


def tick(*args):
    rows, width = args[0].shape[2:]
    depth, cols = args[2].shape[1:]
    if fits(lax.axis_size("dp"), lax.axis_size("seq"), rows, width, depth, cols):
        return one_kernel(*args)
    return per_device(*args)


def solution(mesh):
    return jax.shard_map(
        tick,
        mesh=mesh,
        in_specs=(
            P("section", "dp", "seq", None),
            P("section", "dp", "seq", None),
            P("section", "dp", "seq"),
            P("section", "dp", "seq"),
            P("section", "dp", "seq"),
            P("section", ("seq", "dp"), None),
            P("section", None),
            P(),
            P("section", "dp"),
            P("section", "dp"),
        ),
        out_specs=(P("section", "dp", "seq", None), P("section", "dp", "seq", None)),
        check_vma=False,
    )
```

profile of v0, /device:TPU:30, one launch (start us, length us, event | category | flops | bytes accessed | tf_op | source)
XLA Modules:
  0.0 239.9 jit_solution(16155764483893037034)
XLA Ops:
  1.9 235.7 %shard_map.113 = (bf16[64,4096]{1,0:T(8,128)(2,1)}, bf16[64,4096]{1,0:T(8,128)(2,1)}) custom-call(bf16[64,4096]{1,0:T(8,128)(2,1)} %bitcast.15, bf16[64,4096]{1,0:T(8,128)(2,1)} %bitcast.16, bf16[1024,2048]{1,0:T(8,128)(2,1)} %bitcast.11, bf16[1024,2048]{1,0:T(8,128)(2,1)} %bitcast.12, bf16[1024,2048]{1,0:T(8,128)(2,1)} %bitcast.13, ...), custom_call_target="tpu_custom_call" | custom-call | flops 8589934592 | bytes 16777216 | tf_op jit(solution)/shard_map/pallas_call | solution.py:425
  237.6 2.2 select_bitcast_fusion
where the time goes:
time: 240 us
  Pallas kernels  236 us (98%)
    pallas_call x1, Pallas kernels, one_kernel(): pl.pallas_call(functools.partial(tick_kernel, tuple(vmem) + tuple(sems)),...  236 us

commit v1 on v0

--- a/solution.py
+++ b/solution.py
@@ -91,7 +91,7 @@
 
 ROW_BLOCK = 16
 LANES = 128
-AHEAD = 2
+AHEAD = 3
 OUT_CHUNK = 1024
 VMEM_BYTES = 60 * 1024 * 1024
 BF16 = jnp.bfloat16
@@ -109,14 +109,15 @@
         "other": ((rows, width), BF16),
         "part": ((seqs, seqs, 3, tokens, own), BF16),
         "mine": ((seqs, 3, tokens, own), F32),
-        "got": ((seqs, seqs - 1, 3, tokens, own), BF16),
+        "got": ((seqs, 4, 3, tokens, own), BF16),
+        "far_part": ((2, 3, tokens, own), F32),
         "qkv": ((3, tokens, own), BF16),
         "heads": ((tokens, own), BF16),
         "half": ((seqs, rows, width), F32),
-        "y_out": ((seqs, rows, width), BF16),
-        "y_in": ((seqs, rows, width), BF16),
-        "z_out": ((seqs, rows, width), BF16),
-        "z_in": ((seqs, rows, width), BF16),
+        "y_out": ((seqs, width // OUT_CHUNK, rows, OUT_CHUNK), BF16),
+        "y_in": ((seqs, width // OUT_CHUNK, rows, OUT_CHUNK), BF16),
+        "z_out": ((seqs, width // OUT_CHUNK, rows, OUT_CHUNK), BF16),
+        "z_in": ((seqs, width // OUT_CHUNK, rows, OUT_CHUNK), BF16),
         "late": ((rows, width), BF16),
     }
     sems = {
@@ -124,9 +125,9 @@
         "cut_s": (2, seqs), "cut_r": (2, seqs),
         "fwd_s": (2, seqs), "fwd_r": (2, seqs),
         "bias_s": (seqs,), "bias_r": (seqs,),
-        "part_s": (seqs, seqs - 1), "part_r": (seqs, seqs - 1),
-        "y_s": (seqs,), "y_r": (seqs,),
-        "z_s": (seqs,), "z_r": (seqs,),
+        "part_s": (seqs, 3), "part_r": (seqs, 4),
+        "y_s": (seqs, width // OUT_CHUNK), "y_r": (seqs, width // OUT_CHUNK),
+        "z_s": (seqs, width // OUT_CHUNK), "z_r": (seqs, width // OUT_CHUNK),
         "hand_s": (2,), "hand_r": (2,),
     }
     return vmem, sems
@@ -134,7 +135,7 @@
 
 def fits(seqs, halves, rows, width, depth, cols):
     own = cols // seqs
-    if halves != 2 or rows % ROW_BLOCK or own % LANES or depth % LANES or width % OUT_CHUNK:
+    if seqs != 4 or halves != 2 or rows % ROW_BLOCK or own % LANES or depth % LANES or width % OUT_CHUNK:
         return False
     vmem, _ = scratch_of(seqs, rows, width, depth, cols)
     total = 8 * rows * width * 2
@@ -159,6 +160,10 @@
     section = lax.axis_index("section")
     side = lax.axis_index("seq")
     me = lax.axis_index("dp")
+    near = me + 1 - 2 * lax.rem(me, 2)
+    mirror = seqs - 1 - me
+    far = seqs - 1 - near
+    at_end = 1 - lax.rem(lax.div(me + 1, 2), 2)
     is_first = section == 0
     ahead = lax.rem(section + 1, sections)
     behind = lax.rem(section + sections - 1, sections)
@@ -186,6 +191,16 @@
     ]
     for load in loads:
         load.start()
+
+    @pl.when(at_end == 1)
+    def _():
+        refs["z_in"][mirror] = jnp.zeros((width // OUT_CHUNK, rows, OUT_CHUNK), BF16)
+
+        def clear(b, carry):
+            refs["got"][b, 0] = jnp.zeros((3, tokens, own), BF16)
+            return carry
+
+        lax.fori_loop(0, seqs, clear, 0)
 
     def residual_rows(at):
         return jnp.where(is_first, mem[at, :], act[at, :]).astype(F32)
@@ -234,6 +249,9 @@
             refs["fwd_r"].at[kind, b], {"seq": 1 - side},
         )
 
+    def order(t):
+        return lax.div(t + 3, 4) * (1 + lax.rem(t + 1, 3))
+
     def forward(b):
         @pl.when(b != me)
         def _():
@@ -249,40 +267,76 @@
             for kind in (1, 0):
                 fwd_copy(kind, b, side).start()
 
-    def part_copy(b, step):
-        to = lax.rem(me + step, seqs)
-        return remote(
-            refs["part"].at[b, to], refs["got"].at[b, step - 1], refs["part_s"].at[b, step - 1],
-            refs["part_r"].at[b, step - 1], {"dp": to},
-        )
-
-    def project(b):
+    def part_copy(b, relation):
+        if relation == 0:
+            block, slot = mirror, 3 * at_end
+            device = at_end * near + (1 - at_end) * mirror
+        else:
+            block, slot = (near, far)[relation - 1], relation
+            device = block
+        return remote(
+            refs["part"].at[b, block], refs["got"].at[b, slot], refs["part_s"].at[b, relation],
+            refs["part_r"].at[b, slot], {"dp": device},
+        )
+
+    def part_here(b, slot):
+        return remote(
+            refs["part"].at[b, near], refs["got"].at[b, slot], refs["part_s"].at[b, 1],
+            refs["part_r"].at[b, slot], {"dp": near},
+        )
+
+    def project(t):
+        b = order(t)
         for kind in (1, 0):
             fwd_copy(kind, b, 1 - side).wait_recv()
-        for step in list(range(1, seqs)) + [0]:
-            to = lax.rem(me + step, seqs)
+        for relation, to in enumerate((mirror, near, far, me)):
             at = pl.ds(pl.multiple_of(to * own, own), own)
             for which in range(3):
                 product = jnp.dot(
                     x[min(which, 1), b].reshape(tokens, depth), weights[which, :, at],
                     preferred_element_type=F32,
                 )
-                if step:
+                if relation == 3:
+                    refs["mine"][b, which] = product
+                else:
                     refs["part"][b, to, which] = product.astype(BF16)
-                else:
-                    refs["mine"][b, which] = product
-            if step:
-                part_copy(b, step).start()
-
-    def y_copy(b):
-        return remote(
-            refs["y_out"].at[b], refs["y_in"].at[b], refs["y_s"].at[b], refs["y_r"].at[b],
-            {"seq": 1 - side},
-        )
-
-    def attend_one(b):
-        for step in range(1, seqs):
-            part_copy(b, step).wait_recv()
+                if relation == 2:
+                    refs["far_part"][lax.rem(t, 2), which] = product
+            if relation < 2:
+                part_copy(b, relation).start()
+            elif relation == 2:
+                @pl.when(at_end == 1)
+                def _():
+                    part_copy(b, 2).start()
+
+    def merge(t):
+        b = order(t)
+
+        @pl.when(at_end == 0)
+        def _():
+            part_here(b, 3).wait_recv()
+            for which in range(3):
+                total = refs["far_part"][lax.rem(t, 2), which] + refs["got"][b, 3, which].astype(F32)
+                refs["part"][b, far, which] = total.astype(BF16)
+            part_copy(b, 2).start()
+
+    chunks = width // OUT_CHUNK
+
+    def y_copy(b, c):
+        return remote(
+            refs["y_out"].at[b, c], refs["y_in"].at[b, c], refs["y_s"].at[b, c],
+            refs["y_r"].at[b, c], {"seq": 1 - side},
+        )
+
+    def attend_one(t):
+        b = order(t)
+
+        @pl.when(at_end == 0)
+        def _():
+            part_here(b, 0).wait_recv()
+
+        part_here(b, 1).wait_recv()
+        part_here(b, 2).wait_recv()
 
         @pl.when(b != me)
         def _():
@@ -314,34 +368,53 @@
                 result = out if result is None else jnp.where(inside, out, result)
             refs["heads"][:, at] = result.astype(BF16)
         heads = refs["heads"][...]
-        for start in range(0, width, OUT_CHUNK):
-            at = pl.ds(start, OUT_CHUNK)
+        for c in range(chunks):
+            at = pl.ds(c * OUT_CHUNK, OUT_CHUNK)
             product = jnp.dot(heads, w_out[:, at], preferred_element_type=F32)
             low, high = product[:rows], product[rows:]
             refs["half"][b, :, at] = jnp.where(side == 0, low, high)
-            refs["y_out"][b, :, at] = jnp.where(side == 0, high, low).astype(BF16)
-        y_copy(b).start()
-
-    def z_copy(b):
-        return remote(
-            refs["z_out"].at[b], refs["z_in"].at[me], refs["z_s"].at[b], refs["z_r"].at[me],
-            {"dp": b},
-        )
-
-    def hand_over(b):
-        y_copy(b).wait_recv()
-
-        @pl.when(b != me)
-        def _():
-            refs["z_out"][b] = (refs["half"][b] + refs["y_in"][b].astype(F32)).astype(BF16)
-            z_copy(b).start()
+            refs["y_out"][b, c] = jnp.where(side == 0, high, low).astype(BF16)
+            y_copy(b, c).start()
+
+    def z_copy(b, c, device, slot):
+        return remote(
+            refs["z_out"].at[b, c], refs["z_in"].at[slot, c], refs["z_s"].at[b, c],
+            refs["z_r"].at[slot, c], {"dp": device},
+        )
+
+    def hand_over(t):
+        b = order(t)
+        merged = (b == far) & (at_end == 0)
+        passed = (b == mirror) & (at_end == 1)
+        for c in range(chunks):
+            at = pl.ds(c * OUT_CHUNK, OUT_CHUNK)
+            y_copy(b, c).wait_recv()
+
+            @pl.when((b != me) & jnp.logical_not(merged))
+            def _():
+                total = refs["half"][b, :, at] + refs["y_in"][b, c].astype(F32)
+                refs["z_out"][b, c] = total.astype(BF16)
+
+            @pl.when(merged)
+            def _():
+                z_copy(b, c, near, me).wait_recv()
+                total = refs["half"][b, :, at] + refs["y_in"][b, c].astype(F32)
+                refs["z_out"][b, c] = (total + refs["z_in"][me, c].astype(F32)).astype(BF16)
+
+            @pl.when(passed)
+            def _():
+                z_copy(b, c, near, near).start()
+
+            @pl.when((b != me) & jnp.logical_not(passed))
+            def _():
+                z_copy(b, c, b, me).start()
 
     forward(0)
 
     def turn(t, carry):
         @pl.when(t < seqs - 1)
         def _():
-            forward(t + 1)
+            forward(order(t + 1))
 
         @pl.when(t == 0)
         def _():
@@ -352,6 +425,10 @@
         def _():
             project(t)
 
+        @pl.when((t >= 1) & (t < seqs + 1))
+        def _():
+            merge(t - 1)
+
         @pl.when((t >= AHEAD) & (t < seqs + AHEAD))
         def _():
             attend_one(t - AHEAD)
@@ -364,18 +441,25 @@
 
     lax.fori_loop(0, seqs + AHEAD + 1, turn, 0)
 
-    for step in range(1, seqs):
-        b = lax.rem(me + step, seqs)
-        remote(
-            refs["z_out"].at[b], refs["z_in"].at[b], refs["z_s"].at[b], refs["z_r"].at[b],
-            {"dp": b},
-        ).wait_recv()
+    for c in range(chunks):
+        z_copy(me, c, near, near).wait_recv()
+        z_copy(me, c, far, far).wait_recv()
+
+    @pl.when(at_end == 0)
+    def _():
+        for c in range(chunks):
+            z_copy(me, c, mirror, mirror).wait_recv()
 
     def final_block(r, carry):
         at = pl.ds(pl.multiple_of(r * ROW_BLOCK, ROW_BLOCK), ROW_BLOCK)
-        update = refs["half"][me, at, :] + refs["y_in"][me, at, :].astype(F32)
-        for step in range(1, seqs):
-            update += refs["z_in"][lax.rem(me + step, seqs), at, :].astype(F32)
+        pieces = []
+        for c in range(chunks):
+            piece = refs["half"][me, at, c * OUT_CHUNK:(c + 1) * OUT_CHUNK]
+            piece += refs["y_in"][me, c, at, :].astype(F32)
+            for step in range(1, seqs):
+                piece += refs["z_in"][lax.rem(me + step, seqs), c, at, :].astype(F32)
+            pieces.append(piece)
+        update = jnp.concatenate(pieces, axis=1)
         residual = residual_rows(at)
         place = side * rows + r * ROW_BLOCK + lax.broadcasted_iota(jnp.int32, (ROW_BLOCK, 1), 0)
         kept = jnp.where(place < tgt_len[0, 0], update, jnp.float32(0.0))
@@ -395,14 +479,16 @@
         for kind in range(2):
             cut_copy(kind, b).wait_send()
         bias_copy(b).wait_send()
-        z_copy(b).wait_send()
+        for c in range(chunks):
+            z_copy(b, c, b, me).wait_send()
 
     def drain(b, carry):
         for kind in range(2):
             fwd_copy(kind, b, side).wait_send()
-        for step in range(1, seqs):
-            part_copy(b, step).wait_send()
-        y_copy(b).wait_send()
+        for relation in range(3):
+            part_copy(b, relation).wait_send()
+        for c in range(chunks):
+            y_copy(b, c).wait_send()
         return carry
 
     lax.fori_loop(0, seqs, drain, 0)

time: 240 us -> 179 us (0.75)
  the two profiles are of different devices: /device:TPU:30 before, /device:TPU:8 now
where the time goes in v1:
time: 179 us
  Pallas kernels  175 us (98%)
  other arithmetic  2.24 us (1%)
  between operations  1.94 us (1%)
    pallas_call x1, Pallas kernels, one_kernel(): pl.pallas_call(functools.partial(tick_kernel, tuple(vmem) + tuple(sems)),...  175 us

profile of v1, /device:TPU:8, one launch (start us, length us, event | category | flops | bytes accessed | tf_op | source)
XLA Modules:
  0.0 178.9 jit_solution(6584491189823120993)
XLA Ops:
  1.9 174.7 %shard_map.113 = (bf16[64,4096]{1,0:T(8,128)(2,1)}, bf16[64,4096]{1,0:T(8,128)(2,1)}) custom-call(bf16[64,4096]{1,0:T(8,128)(2,1)} %bitcast.15, bf16[64,4096]{1,0:T(8,128)(2,1)} %bitcast.16, bf16[1024,2048]{1,0:T(8,128)(2,1)} %bitcast.11, bf16[1024,2048]{1,0:T(8,128)(2,1)} %bitcast.12, bf16[1024,2048]{1,0:T(8,128)(2,1)} %bitcast.13, ...), custom_call_target="tpu_custom_call" | custom-call | flops 8589934592 | bytes 16777216 | tf_op jit(solution)/shard_map/pallas_call | solution.py:511
  176.7 2.2 %select_bitcast_fusion = (bf16[1,1,64,4096]{3,2,1,0:T(8,128)(2,1)}, bf16[1,1,64,4096]{3,2,1,0:T(8,128)(2,1)}) fusion(bf16[64,4096]{1,0:T(8,128)(2,1)} %get-tuple-element.5, bf16[64,4096]{1,0:T(8,128)(2,1)} %get-tuple-element.4, pred[]{:T(512)S(6)} %eq.3), kind=kLoop, calls=%fused_computation | loop fusion | flops 524288 | bytes 2097153 | tf_op jit(solution)/shard_map/broadcast_in_dim | solution.py:531

commit v2 on v1

--- a/solution.py
+++ b/solution.py
@@ -92,7 +92,7 @@
 ROW_BLOCK = 16
 LANES = 128
 AHEAD = 3
-OUT_CHUNK = 1024
+OUT_CHUNK = 512
 VMEM_BYTES = 60 * 1024 * 1024
 BF16 = jnp.bfloat16
 F32 = jnp.float32

time: 179 us -> 178 us (level)
  Pallas kernels: 175 us -> 173 us
where the time goes in v2:
time: 178 us
  Pallas kernels  173 us (97%)
  other arithmetic  2.24 us (1%)
  between operations  1.94 us (1%)
    pallas_call x1, Pallas kernels, one_kernel(): pl.pallas_call(functools.partial(tick_kernel, tuple(vmem) + tuple(sems)),...  173 us

profile of v2, /device:TPU:8, one launch (start us, length us, event | category | flops | bytes accessed | tf_op | source)
XLA Modules:
  0.0 177.6 jit_solution(8036200421084587354)
XLA Ops:
  1.9 173.4 %shard_map.113 = (bf16[64,4096]{1,0:T(8,128)(2,1)}, bf16[64,4096]{1,0:T(8,128)(2,1)}) custom-call(bf16[64,4096]{1,0:T(8,128)(2,1)} %bitcast.15, bf16[64,4096]{1,0:T(8,128)(2,1)} %bitcast.16, bf16[1024,2048]{1,0:T(8,128)(2,1)} %bitcast.11, bf16[1024,2048]{1,0:T(8,128)(2,1)} %bitcast.12, bf16[1024,2048]{1,0:T(8,128)(2,1)} %bitcast.13, ...), custom_call_target="tpu_custom_call" | custom-call | flops 8589934592 | bytes 16777216 | tf_op jit(solution)/shard_map/pallas_call | solution.py:511
  175.3 2.2 %select_bitcast_fusion = (bf16[1,1,64,4096]{3,2,1,0:T(8,128)(2,1)}, bf16[1,1,64,4096]{3,2,1,0:T(8,128)(2,1)}) fusion(bf16[64,4096]{1,0:T(8,128)(2,1)} %get-tuple-element.5, bf16[64,4096]{1,0:T(8,128)(2,1)} %get-tuple-element.4, pred[]{:T(512)S(6)} %eq.3), kind=kLoop, calls=%fused_computation | loop fusion | flops 524288 | bytes 2097153 | tf_op jit(solution)/shard_map/broadcast_in_dim | solution.py:531
